TPU v7x, 32 devices: a whole 2x2x4 slice. The times are simulated.
32 devices in a mesh: section: 4 (over y, x), fsdp: 8 (over z, core).
Axes of the slice: x: 2, y: 2, z: 4, core: 2. Of those that a mesh axis runs over, the one named last changes fastest.
Arguments:
- inputs: bfloat16 [8, 128, 8192], P(None, 'fsdp'), may hold values from -6 to 6
- cotangent: bfloat16 [8, 128, 8192], P(None, 'fsdp'), may hold values from -6 to 6
- kv_weight: bfloat16 [4, 8192, 1024], P('section', 'fsdp'), may hold values from -0.0625 to 0.0625
- norm_gain: bfloat16 [4, 8192], P('section', 'fsdp'), may hold values from 0.25 to 1.75
Outputs:
- kv_grad: float32 [4, 8192, 1024], P('section', 'fsdp')
- gain_grad: float32 [4, 8192], P('section', 'fsdp')
All inputs are finite; a program needn't handle non-finite values.
Results may differ from a plain program's by a relative error of at most 0.02.
Values may be sent and summed in bfloat16 or wider, within the bound.
A program may use at most 128 MiB of HBM per device.

v0:
```python
from functools import partial

import jax
import jax.numpy as jnp
from jax import lax
from jax.sharding import PartitionSpec as P

HD = 128
KVH = 4


epsilon = 1e-05


def from_behind(shard, axis, by):
    devices = lax.axis_size(axis)
    pairs = [(i, i + by) for i in range(devices) if 0 <= i + by < devices]
    return lax.ppermute(shard, axis, pairs)


def normalize(rows_f32, gain_f32):
    mean_sq = jnp.mean(rows_f32 * rows_f32, axis=-1, keepdims=True)
    return rows_f32 * lax.rsqrt(mean_sq + epsilon) * gain_f32


def attend(normed, keyval, kv_heads, head_size):
    batch_size, length, model_width = normed.shape
    group = model_width // head_size // kv_heads
    kv_width = kv_heads * head_size
    queries = normed.reshape(batch_size, length, kv_heads, group, head_size).astype(jnp.float32)
    keys = (
        keyval[:, :, :kv_width].reshape(batch_size, length, kv_heads, head_size).astype(jnp.float32)
    )
    values = (
        keyval[:, :, kv_width:].reshape(batch_size, length, kv_heads, head_size).astype(jnp.float32)
    )
    scores = jnp.einsum("blkgd,bmkd->bkglm", queries, keys) * head_size ** (-0.5)
    position = jnp.arange(length)
    causal_mask = position[:, None] >= position[None, :]
    scores = jnp.where(causal_mask, scores, -1e30)
    largest = jnp.max(scores, axis=-1, keepdims=True)
    exponent_terms = jnp.exp(scores - largest)
    attn_weights = (exponent_terms / jnp.sum(exponent_terms, axis=-1, keepdims=True)).astype(
        jnp.bfloat16
    )
    mixed = jnp.einsum("bkglm,bmkd->blkgd", attn_weights.astype(jnp.float32), values)
    return mixed.reshape(batch_size, length, model_width)


def project(normed, weight):
    batch_size, length, model_width = normed.shape
    flat_rows = normed.reshape(batch_size * length, model_width)
    keyval = jnp.dot(flat_rows, weight, preferred_element_type=jnp.float32).astype(jnp.bfloat16)
    return keyval.reshape(batch_size, length, weight.shape[1])


def forward_layer(rows, gain_row, weight, kv_heads, head_size):
    normed = normalize(rows.astype(jnp.float32), gain_row.astype(jnp.float32)).astype(jnp.bfloat16)
    keyval = project(normed, weight)
    mixed = attend(normed, keyval, kv_heads, head_size)
    return ((rows.astype(jnp.float32) + mixed).astype(jnp.bfloat16), keyval)


def backward_layer(rows, keyval, gain_row, weight, grad_out, kv_heads, head_size):
    batch_size, length, model_width = rows.shape
    rows_f32 = rows.astype(jnp.float32)
    normed_f32, norm_pull = jax.vjp(normalize, rows_f32, gain_row.astype(jnp.float32))
    normed = normed_f32.astype(jnp.bfloat16)
    mixed, attend_pull = jax.vjp(
        partial(attend, kv_heads=kv_heads, head_size=head_size), normed, keyval
    )
    d_normed, d_keyval = attend_pull(grad_out.astype(jnp.float32))
    flat_dkv = d_keyval.reshape(batch_size * length, weight.shape[1])
    back = lax.dot_general(
        flat_dkv, weight, (((1,), (1,)), ((), ())), preferred_element_type=jnp.float32
    )
    d_total = d_normed.astype(jnp.float32) + back.reshape(batch_size, length, model_width)
    d_rows_f32, unused_gain = norm_pull(d_total)
    inverse = lax.rsqrt(jnp.mean(rows_f32 * rows_f32, axis=-1, keepdims=True) + epsilon)
    gain_rows = d_total * (rows_f32 * inverse)
    d_rows = (grad_out.astype(jnp.float32) + d_rows_f32).astype(jnp.bfloat16)
    return (d_rows, normed, d_keyval, gain_rows)


def local(inputs, cotangent, kv_weight, norm_gain):
    section_count = lax.axis_size("section")
    section_index = lax.axis_index("section")
    micro_count = inputs.shape[0]
    seq_length = inputs.shape[1]
    model_width = inputs.shape[2]
    kv_cols = kv_weight.shape[2]
    head_size = HD
    kv_heads = KVH
    round_count = micro_count + section_count - 1
    weight_full, gain_full = (
        lax.all_gather(kv_weight, "fsdp", axis=1, tiled=True),
        lax.all_gather(norm_gain, "fsdp", axis=1, tiled=True),
    )
    weight = weight_full[0]
    gain_row = gain_full[0]

    def forward_round(carry, step_index):
        incoming, saved_rows, saved_kv = carry
        micro_pos = step_index - section_index
        is_valid = (micro_pos >= 0) & (micro_pos < micro_count)
        slot_index = jnp.clip(micro_pos, 0, micro_count - 1)
        fresh_rows = lax.dynamic_index_in_dim(
            inputs, jnp.clip(step_index, 0, micro_count - 1), 0, keepdims=True
        )
        layer_in = jnp.where(section_index == 0, fresh_rows, incoming)

        def forward_active(operands):
            rows, kept_rows, kept_kv = operands
            layer_out, keyval = forward_layer(rows, gain_row, weight, kv_heads, head_size)
            kept_rows = lax.dynamic_update_index_in_dim(kept_rows, rows, slot_index, 0)
            kept_kv = lax.dynamic_update_index_in_dim(kept_kv, keyval, slot_index, 0)
            return (layer_out, kept_rows, kept_kv)

        def forward_resting(operands):
            rows, kept_rows, kept_kv = operands
            return (jnp.zeros_like(rows), kept_rows, kept_kv)

        layer_out, saved_rows, saved_kv = lax.cond(
            is_valid, forward_active, forward_resting, (layer_in, saved_rows, saved_kv)
        )
        incoming = from_behind(layer_out, "section", 1)
        return ((incoming, saved_rows, saved_kv), None)

    start_rows = jnp.zeros((1, seq_length, model_width), jnp.bfloat16)
    rows_start = jnp.zeros((micro_count, seq_length, model_width), jnp.bfloat16)
    kv_start = jnp.zeros((micro_count, seq_length, kv_cols), jnp.bfloat16)
    (unused_rows, saved_rows, saved_kv), unused_out = lax.scan(
        forward_round, (start_rows, rows_start, kv_start), jnp.arange(round_count)
    )

    def backward_round(carry, step_index):
        incoming, normed_store, dkv_store, gain_accum = carry
        micro_pos = step_index - (section_count - 1 - section_index)
        is_valid = (micro_pos >= 0) & (micro_pos < micro_count)
        slot_index = jnp.clip(micro_pos, 0, micro_count - 1)
        fresh_grad = lax.dynamic_index_in_dim(
            cotangent, jnp.clip(step_index, 0, micro_count - 1), 0, keepdims=True
        )
        grad_in = jnp.where(section_index == section_count - 1, fresh_grad, incoming)

        def backward_active(operands):
            grad_rows, kept_normed, kept_dkv, kept_gain = operands
            rows = lax.dynamic_index_in_dim(saved_rows, slot_index, 0, keepdims=True)
            keyval = lax.dynamic_index_in_dim(saved_kv, slot_index, 0, keepdims=True)
            d_rows, normed, d_keyval, gain_rows = backward_layer(
                rows, keyval, gain_row, weight, grad_rows, kv_heads, head_size
            )
            kept_normed = lax.dynamic_update_index_in_dim(kept_normed, normed, slot_index, 0)
            kept_dkv = lax.dynamic_update_index_in_dim(kept_dkv, d_keyval, slot_index, 0)
            kept_gain = kept_gain + jnp.sum(gain_rows, axis=(0, 1))
            return (d_rows, kept_normed, kept_dkv, kept_gain)

        def backward_resting(operands):
            grad_rows, kept_normed, kept_dkv, kept_gain = operands
            return (jnp.zeros_like(grad_rows), kept_normed, kept_dkv, kept_gain)

        d_rows, normed_store, dkv_store, gain_accum = lax.cond(
            is_valid,
            backward_active,
            backward_resting,
            (grad_in, normed_store, dkv_store, gain_accum),
        )
        incoming = from_behind(d_rows, "section", -1)
        return ((incoming, normed_store, dkv_store, gain_accum), None)

    gain_start = jnp.zeros((model_width,), jnp.float32)
    (unused_grad, normed_store, dkv_store, gain_accum), unused_back = lax.scan(
        backward_round, (start_rows, rows_start, kv_start, gain_start), jnp.arange(round_count)
    )
    normed_all = normed_store.reshape(micro_count * seq_length, model_width)
    dkv_all = dkv_store.reshape(micro_count * seq_length, kv_cols)
    w_term = lax.dot_general(
        normed_all, dkv_all, (((0,), (0,)), ((), ())), preferred_element_type=jnp.float32
    )
    w_share, g_share = (
        lax.psum_scatter(
            w_term.astype(jnp.bfloat16), "fsdp", scatter_dimension=0, tiled=True
        ).astype(jnp.float32),
        lax.psum_scatter(
            gain_accum.astype(jnp.bfloat16), "fsdp", scatter_dimension=0, tiled=True
        ).astype(jnp.float32),
    )
    return (w_share[None], g_share[None])


def solution(mesh):
    in_specs = (
        P(None, "fsdp", None),
        P(None, "fsdp", None),
        P("section", "fsdp", None),
        P("section", "fsdp"),
    )
    out_specs = (P("section", "fsdp", None), P("section", "fsdp"))
    return jax.shard_map(local, mesh=mesh, in_specs=in_specs, out_specs=out_specs, check_vma=False)
```

profile of v0, /device:TPU:0, one launch (start us, length us, event | category | flops | bytes accessed | tf_op | source)
XLA Modules:
  0.0 1037.1 jit_solution(18444544215524454594)
XLA Ops:
  8.0 15.7 %all_gather.6 = bf16[1,8192]{1,0:T(2,128)(2,1)S(1)} all-gather(bf16[1,1024]{1,0:T(2,128)(2,1)S(1)} %copy-done.7), channel_id=1, replica_groups=mesh['section'=4,'fsdp'=8] {'fsdp'}, dimensions={1}, use_global_device_ids=true | all-gather | bytes 18432 | tf_op jit(solution)/shard_map/all_gather | solution.py:97
  24.3 139.1 %all-gather.2.cloned.1.call-done = bf16[1,8192,1024]{2,1,0:T(8,128)(2,1)} async-done(((bf16[1,1024,1024]{2,1,0:T(8,128)(2,1)}), bf16[1,8192,1024]{2,1,0:T(8,128)(2,1)}) %all-gather.2.cloned.1.call-update) | async-done | bytes 16777232 | tf_op jit(solution)/shard_map/all_gather | solution.py:96
  164.4 248.3 %while.33 = (s32[]{:T(128)}, bf16[1,16,8192]{2,1,0:T(8,128)(2,1)S(1)}, bf16[8,16,8192]{2,1,0:T(8,128)(2,1)S(1)}, bf16[8,16,1024]{2,1,0:T(8,128)(2,1)}, s32[11]{0...) while((s32[]{:T(128)}, ...), condition=%wide.region_6.7_spmd, body=%wide.region_0.6_spmd.sunk | while | flops 278944032 | bytes 24024260 | solution.py:132
  165.6 13.5 %conditional.4 = (bf16[1,16,8192]{2,1,0:T(8,128)(2,1)S(1)}, bf16[8,16,8192]{2,1,0:T(8,128)(2,1)S(1)}, bf16[8,16,1024]{2,1,0:T(8,128)(2,1)}) conditional(s32[]{:T(128)} %convert_element_type.239, (bf16[8,16,8192]{2,1,0:T(8,128)(2,1)S(1)}, bf16[8,16,1024]{2,1,0:T(8,128)(2,1)}) %tuple.96, (pred[]{:T(512)}, s32[]{:T(128)}, ...), branch_computations={%region_1.1_spmd, %region_2.5_spmd} | conditional | flops 278944032 | bytes 22975380 | solution.py:123
  168.1 8.7 constant_dynamic-update-slice_fusion.1
  180.4 6.2 collective-permute-done
  187.8 13.5 %conditional.4 = (bf16[1,16,8192]{2,1,0:T(8,128)(2,1)S(1)}, bf16[8,16,8192]{2,1,0:T(8,128)(2,1)S(1)}, bf16[8,16,1024]{2,1,0:T(8,128)(2,1)}) conditional(s32[]{:T(128)} %convert_element_type.239, (bf16[8,16,8192]{2,1,0:T(8,128)(2,1)S(1)}, bf16[8,16,1024]{2,1,0:T(8,128)(2,1)}) %tuple.96, (pred[]{:T(512)}, s32[]{:T(128)}, ...), branch_computations={%region_1.1_spmd, %region_2.5_spmd} | conditional | flops 278944032 | bytes 22975380 | solution.py:123
  190.3 8.7 constant_dynamic-update-slice_fusion.1
  201.3 4.4 collective-permute-start
  205.7 5.5 collective-permute-done
  212.3 13.5 %conditional.4 = (bf16[1,16,8192]{2,1,0:T(8,128)(2,1)S(1)}, bf16[8,16,8192]{2,1,0:T(8,128)(2,1)S(1)}, bf16[8,16,1024]{2,1,0:T(8,128)(2,1)}) conditional(s32[]{:T(128)} %convert_element_type.239, (bf16[8,16,8192]{2,1,0:T(8,128)(2,1)S(1)}, bf16[8,16,1024]{2,1,0:T(8,128)(2,1)}) %tuple.96, (pred[]{:T(512)}, s32[]{:T(128)}, ...), branch_computations={%region_1.1_spmd, %region_2.5_spmd} | conditional | flops 278944032 | bytes 22975380 | solution.py:123
  214.8 8.7 constant_dynamic-update-slice_fusion.1
  225.8 4.4 collective-permute-start
  230.2 4.6 collective-permute-done
  235.9 13.5 %conditional.4 = (bf16[1,16,8192]{2,1,0:T(8,128)(2,1)S(1)}, bf16[8,16,8192]{2,1,0:T(8,128)(2,1)S(1)}, bf16[8,16,1024]{2,1,0:T(8,128)(2,1)}) conditional(s32[]{:T(128)} %convert_element_type.239, (bf16[8,16,8192]{2,1,0:T(8,128)(2,1)S(1)}, bf16[8,16,1024]{2,1,0:T(8,128)(2,1)}) %tuple.96, (pred[]{:T(512)}, s32[]{:T(128)}, ...), branch_computations={%region_1.1_spmd, %region_2.5_spmd} | conditional | flops 278944032 | bytes 22975380 | solution.py:123
  238.4 8.7 constant_dynamic-update-slice_fusion.1
  249.4 4.4 collective-permute-start
  258.8 13.5 %conditional.4 = (bf16[1,16,8192]{2,1,0:T(8,128)(2,1)S(1)}, bf16[8,16,8192]{2,1,0:T(8,128)(2,1)S(1)}, bf16[8,16,1024]{2,1,0:T(8,128)(2,1)}) conditional(s32[]{:T(128)} %convert_element_type.239, (bf16[8,16,8192]{2,1,0:T(8,128)(2,1)S(1)}, bf16[8,16,1024]{2,1,0:T(8,128)(2,1)}) %tuple.96, (pred[]{:T(512)}, s32[]{:T(128)}, ...), branch_computations={%region_1.1_spmd, %region_2.5_spmd} | conditional | flops 278944032 | bytes 22975380 | solution.py:123
  261.4 8.7 constant_dynamic-update-slice_fusion.1
  272.3 4.4 collective-permute-start
  281.8 13.5 %conditional.4 = (bf16[1,16,8192]{2,1,0:T(8,128)(2,1)S(1)}, bf16[8,16,8192]{2,1,0:T(8,128)(2,1)S(1)}, bf16[8,16,1024]{2,1,0:T(8,128)(2,1)}) conditional(s32[]{:T(128)} %convert_element_type.239, (bf16[8,16,8192]{2,1,0:T(8,128)(2,1)S(1)}, bf16[8,16,1024]{2,1,0:T(8,128)(2,1)}) %tuple.96, (pred[]{:T(512)}, s32[]{:T(128)}, ...), branch_computations={%region_1.1_spmd, %region_2.5_spmd} | conditional | flops 278944032 | bytes 22975380 | solution.py:123
  284.3 8.7 constant_dynamic-update-slice_fusion.1
  295.3 5.3 collective-permute-start
  305.6 13.5 %conditional.4 = (bf16[1,16,8192]{2,1,0:T(8,128)(2,1)S(1)}, bf16[8,16,8192]{2,1,0:T(8,128)(2,1)S(1)}, bf16[8,16,1024]{2,1,0:T(8,128)(2,1)}) conditional(s32[]{:T(128)} %convert_element_type.239, (bf16[8,16,8192]{2,1,0:T(8,128)(2,1)S(1)}, bf16[8,16,1024]{2,1,0:T(8,128)(2,1)}) %tuple.96, (pred[]{:T(512)}, s32[]{:T(128)}, ...), branch_computations={%region_1.1_spmd, %region_2.5_spmd} | conditional | flops 278944032 | bytes 22975380 | solution.py:123
  308.1 8.7 constant_dynamic-update-slice_fusion.1
  319.1 5.3 collective-permute-start
  329.4 13.5 %conditional.4 = (bf16[1,16,8192]{2,1,0:T(8,128)(2,1)S(1)}, bf16[8,16,8192]{2,1,0:T(8,128)(2,1)S(1)}, bf16[8,16,1024]{2,1,0:T(8,128)(2,1)}) conditional(s32[]{:T(128)} %convert_element_type.239, (bf16[8,16,8192]{2,1,0:T(8,128)(2,1)S(1)}, bf16[8,16,1024]{2,1,0:T(8,128)(2,1)}) %tuple.96, (pred[]{:T(512)}, s32[]{:T(128)}, ...), branch_computations={%region_1.1_spmd, %region_2.5_spmd} | conditional | flops 278944032 | bytes 22975380 | solution.py:123
  331.9 8.7 constant_dynamic-update-slice_fusion.1
  342.9 5.3 collective-permute-start
  353.3 18.7 %collective-permute-start = (bf16[1,16,8192]{2,1,0:T(8,128)(2,1)S(1)}, bf16[1,16,8192]{2,1,0:T(8,128)(2,1)S(1)}, u32[]{:S(2)}, u32[]{:S(2)}) collective-permute-start(bf16[1,16,8192]{2,1,0:T(8,128)(2,1)S(1)} %get-tuple-element.690), channel_id=1, source_target_pairs={{0,8},{8,16},{16,24},{1,9},{9,17},{17,25},{2,10},{10,18},{18,26},{... | collective-permute-start | bytes 786440 | tf_op jit(solution)/shard_map/while/body/eval_jaxpr/ppermute | solution.py:18
  372.0 5.3 collective-permute-done
  378.5 4.4 collective-permute-start
  388.0 20.9 %collective-permute-start = (bf16[1,16,8192]{2,1,0:T(8,128)(2,1)S(1)}, bf16[1,16,8192]{2,1,0:T(8,128)(2,1)S(1)}, u32[]{:S(2)}, u32[]{:S(2)}) collective-permute-start(bf16[1,16,8192]{2,1,0:T(8,128)(2,1)S(1)} %get-tuple-element.690), channel_id=1, source_target_pairs={{0,8},{8,16},{16,24},{1,9},{9,17},{17,25},{2,10},{10,18},{18,26},{... | collective-permute-start | bytes 786440 | tf_op jit(solution)/shard_map/while/body/eval_jaxpr/ppermute | solution.py:18
  416.1 432.8 %while.34 = (s32[]{:T(128)}, bf16[1,16,8192]{2,1,0:T(8,128)(2,1)S(1)}, bf16[8,16,8192]{2,1,0:T(8,128)(2,1)}, bf16[8,16,1024]{2,1,0:T(8,128)(2,1)}, f32[8192]{0:T...) while((s32[]{:T(128)}, ...), condition=%wide.region_18.19_spmd, body=%wide.region_7.18_spmd.sunk | while | flops 294109568 | bytes 29291696 | solution.py:172
  419.9 10.5 %collective-permute-done.1 = bf16[1,16,8192]{2,1,0:T(8,128)(2,1)S(1)} collective-permute-done((bf16[1,16,8192]{2,1,0:T(8,128)(2,1)}, bf16[1,16,8192]{2,1,0:T(8,128)(2,1)S(1)}, u32[]{:S(2)}, u32[]{:S(2)}) %collective-permute-start.1) | collective-permute-done | bytes 262176 | tf_op jit(solution)/shard_map/while/body/eval_jaxpr/ppermute | solution.py:18
  434.3 14.7 %collective-permute-done.1 = bf16[1,16,8192]{2,1,0:T(8,128)(2,1)S(1)} collective-permute-done((bf16[1,16,8192]{2,1,0:T(8,128)(2,1)}, bf16[1,16,8192]{2,1,0:T(8,128)(2,1)S(1)}, u32[]{:S(2)}, u32[]{:S(2)}) %collective-permute-start.1) | collective-permute-done | bytes 262176 | tf_op jit(solution)/shard_map/while/body/eval_jaxpr/ppermute | solution.py:18
  452.8 87.5 %collective-permute-done.1 = bf16[1,16,8192]{2,1,0:T(8,128)(2,1)S(1)} collective-permute-done((bf16[1,16,8192]{2,1,0:T(8,128)(2,1)}, bf16[1,16,8192]{2,1,0:T(8,128)(2,1)S(1)}, u32[]{:S(2)}, u32[]{:S(2)}) %collective-permute-start.1) | collective-permute-done | bytes 262176 | tf_op jit(solution)/shard_map/while/body/eval_jaxpr/ppermute | solution.py:18
  542.0 27.5 %conditional.5 = (bf16[1,16,8192]{2,1,0:T(8,128)(2,1)}, bf16[8,16,8192]{2,1,0:T(8,128)(2,1)}, bf16[8,16,1024]{2,1,0:T(8,128)(2,1)}, f32[8192]{0:T(1024)}) conditional(s32[]{:T(128)} %convert_element_type.240, (bf16[8,16,8192]{2,1,0:T(8,128)(2,1)}, bf16[8,16,1024]{2,1,0:T(8,128)(2,1)}, f32[8192]{0:T(1024)}) %tuple.99, (pred[]{:T(512)}, s32[]{:T(128)}, ...), branch_computations={%region_8.8_spmd, %region_9.17_spmd} | conditional | flops 294109568 | bytes 28242760 | solution.py:162
  555.2 10.3 fusion.28
  570.9 8.1 collective-permute-done.1
  580.7 27.6 %conditional.5 = (bf16[1,16,8192]{2,1,0:T(8,128)(2,1)}, bf16[8,16,8192]{2,1,0:T(8,128)(2,1)}, bf16[8,16,1024]{2,1,0:T(8,128)(2,1)}, f32[8192]{0:T(1024)}) conditional(s32[]{:T(128)} %convert_element_type.240, (bf16[8,16,8192]{2,1,0:T(8,128)(2,1)}, bf16[8,16,1024]{2,1,0:T(8,128)(2,1)}, f32[8192]{0:T(1024)}) %tuple.99, (pred[]{:T(512)}, s32[]{:T(128)}, ...), branch_computations={%region_8.8_spmd, %region_9.17_spmd} | conditional | flops 294109568 | bytes 28242760 | solution.py:162
  593.9 10.3 fusion.28
  609.6 8.1 collective-permute-done.1
  619.4 27.6 %conditional.5 = (bf16[1,16,8192]{2,1,0:T(8,128)(2,1)}, bf16[8,16,8192]{2,1,0:T(8,128)(2,1)}, bf16[8,16,1024]{2,1,0:T(8,128)(2,1)}, f32[8192]{0:T(1024)}) conditional(s32[]{:T(128)} %convert_element_type.240, (bf16[8,16,8192]{2,1,0:T(8,128)(2,1)}, bf16[8,16,1024]{2,1,0:T(8,128)(2,1)}, f32[8192]{0:T(1024)}) %tuple.99, (pred[]{:T(512)}, s32[]{:T(128)}, ...), branch_computations={%region_8.8_spmd, %region_9.17_spmd} | conditional | flops 294109568 | bytes 28242760 | solution.py:162
  632.5 10.3 fusion.28
  648.3 8.1 collective-permute-done.1
  658.1 27.6 %conditional.5 = (bf16[1,16,8192]{2,1,0:T(8,128)(2,1)}, bf16[8,16,8192]{2,1,0:T(8,128)(2,1)}, bf16[8,16,1024]{2,1,0:T(8,128)(2,1)}, f32[8192]{0:T(1024)}) conditional(s32[]{:T(128)} %convert_element_type.240, (bf16[8,16,8192]{2,1,0:T(8,128)(2,1)}, bf16[8,16,1024]{2,1,0:T(8,128)(2,1)}, f32[8192]{0:T(1024)}) %tuple.99, (pred[]{:T(512)}, s32[]{:T(128)}, ...), branch_computations={%region_8.8_spmd, %region_9.17_spmd} | conditional | flops 294109568 | bytes 28242760 | solution.py:162
  671.2 10.3 fusion.28
  687.0 8.1 collective-permute-done.1
  696.8 27.6 %conditional.5 = (bf16[1,16,8192]{2,1,0:T(8,128)(2,1)}, bf16[8,16,8192]{2,1,0:T(8,128)(2,1)}, bf16[8,16,1024]{2,1,0:T(8,128)(2,1)}, f32[8192]{0:T(1024)}) conditional(s32[]{:T(128)} %convert_element_type.240, (bf16[8,16,8192]{2,1,0:T(8,128)(2,1)}, bf16[8,16,1024]{2,1,0:T(8,128)(2,1)}, f32[8192]{0:T(1024)}) %tuple.99, (pred[]{:T(512)}, s32[]{:T(128)}, ...), branch_computations={%region_8.8_spmd, %region_9.17_spmd} | conditional | flops 294109568 | bytes 28242760 | solution.py:162
  709.9 10.3 fusion.28
  725.7 8.1 collective-permute-done.1
  735.5 27.6 %conditional.5 = (bf16[1,16,8192]{2,1,0:T(8,128)(2,1)}, bf16[8,16,8192]{2,1,0:T(8,128)(2,1)}, bf16[8,16,1024]{2,1,0:T(8,128)(2,1)}, f32[8192]{0:T(1024)}) conditional(s32[]{:T(128)} %convert_element_type.240, (bf16[8,16,8192]{2,1,0:T(8,128)(2,1)}, bf16[8,16,1024]{2,1,0:T(8,128)(2,1)}, f32[8192]{0:T(1024)}) %tuple.99, (pred[]{:T(512)}, s32[]{:T(128)}, ...), branch_computations={%region_8.8_spmd, %region_9.17_spmd} | conditional | flops 294109568 | bytes 28242760 | solution.py:162
  748.6 10.3 fusion.28
  764.3 8.1 collective-permute-done.1
  774.2 27.5 %conditional.5 = (bf16[1,16,8192]{2,1,0:T(8,128)(2,1)}, bf16[8,16,8192]{2,1,0:T(8,128)(2,1)}, bf16[8,16,1024]{2,1,0:T(8,128)(2,1)}, f32[8192]{0:T(1024)}) conditional(s32[]{:T(128)} %convert_element_type.240, (bf16[8,16,8192]{2,1,0:T(8,128)(2,1)}, bf16[8,16,1024]{2,1,0:T(8,128)(2,1)}, f32[8192]{0:T(1024)}) %tuple.99, (pred[]{:T(512)}, s32[]{:T(128)}, ...), branch_computations={%region_8.8_spmd, %region_9.17_spmd} | conditional | flops 294109568 | bytes 28242760 | solution.py:162
  787.3 10.3 fusion.28
  803.0 8.1 collective-permute-done.1
  812.9 27.6 %conditional.5 = (bf16[1,16,8192]{2,1,0:T(8,128)(2,1)}, bf16[8,16,8192]{2,1,0:T(8,128)(2,1)}, bf16[8,16,1024]{2,1,0:T(8,128)(2,1)}, f32[8192]{0:T(1024)}) conditional(s32[]{:T(128)} %convert_element_type.240, (bf16[8,16,8192]{2,1,0:T(8,128)(2,1)}, bf16[8,16,1024]{2,1,0:T(8,128)(2,1)}, f32[8192]{0:T(1024)}) %tuple.99, (pred[]{:T(512)}, s32[]{:T(128)}, ...), branch_computations={%region_8.8_spmd, %region_9.17_spmd} | conditional | flops 294109568 | bytes 28242760 | solution.py:162
  826.0 10.4 fusion.28
  841.7 7.2 collective-permute-done.1
  848.9 11.9 %bitcast_convert_fusion = bf16[8192,1024]{1,0:T(8,128)(2,1)} fusion(bf16[8,16,8192]{2,1,0:T(8,128)(2,1)} %get-tuple-element.459, bf16[8,16,1024]{2,1,0:T(8,128)(2,1)} %get-tuple-element.460), kind=kOutput, calls=%fused_computation.92 | convolution fusion | flops 2155872256 | bytes 19136512 | tf_op jit(solution)/shard_map/dot_general | solution.py:177
  863.4 27.2 %all-reduce.2 = bf16[8192]{0:T(1024)(128)(2,1)S(1)} all-reduce(bf16[8192]{0:T(1024)(128)(2,1)S(1)} %convert_element_type.149), channel_id=3, replica_groups=mesh['section'=4,'fsdp'=8] {'fsdp'}, use_global_device_ids=true, to_apply=%region_20.21.clone | all-reduce | flops 8192 | bytes 32768
  891.2 135.0 %reduce-scatter.2.cloned.1.call-done = bf16[1024,1024]{1,0:T(8,128)(2,1)} async-done(((bf16[8192,1024]{1,0:T(8,128)(2,1)}), bf16[1024,1024]{1,0:T(8,128)(2,1)}) %reduce-scatter.2.cloned.1.call-update) | async-done | bytes 2097168 | tf_op jit(solution)/shard_map/reduce_scatter | solution.py:181
  (579 shorter events, 243.3 us)
Async XLA Ops:
  7.2 0.8 copy-start.7
  7.2 156.3 %all-gather.2.cloned.1.call-start = ((), (), s32[]{:S(2)}) async-start(), calls=%async_computation.1 | async-start | bytes 18874368 | tf_op jit(solution)/shard_map/all_gather | solution.py:96
  7.9 1018.3 %reduce-scatter.2.cloned.1.call-start = ((), (), s32[]{:S(2)}) async-start(), calls=%async_computation.2 | async-start | bytes 18874368 | tf_op jit(solution)/shard_map/reduce_scatter | solution.py:181
  179.1 7.5 collective-permute-start
  201.3 9.9 collective-permute-start
  225.8 9.0 collective-permute-start
  249.4 8.3 collective-permute-start
  272.3 8.3 collective-permute-start
  295.3 9.2 collective-permute-start
  319.1 9.2 collective-permute-start
  342.9 9.2 collective-permute-start
  353.3 24.0 %collective-permute-start = (bf16[1,16,8192]{2,1,0:T(8,128)(2,1)S(1)}, bf16[1,16,8192]{2,1,0:T(8,128)(2,1)S(1)}, u32[]{:S(2)}, u32[]{:S(2)}) collective-permute-start(bf16[1,16,8192]{2,1,0:T(8,128)(2,1)S(1)} %get-tuple-element.690), channel_id=1, source_target_pairs={{0,8},{8,16},{16,24},{1,9},{9,17},{17,25},{2,10},{10,18},{18,26},{... | collective-permute-start | bytes 786440 | tf_op jit(solution)/shard_map/while/body/eval_jaxpr/ppermute | solution.py:18
  378.5 8.3 collective-permute-start
  388.0 24.7 %collective-permute-start = (bf16[1,16,8192]{2,1,0:T(8,128)(2,1)S(1)}, bf16[1,16,8192]{2,1,0:T(8,128)(2,1)S(1)}, u32[]{:S(2)}, u32[]{:S(2)}) collective-permute-start(bf16[1,16,8192]{2,1,0:T(8,128)(2,1)S(1)} %get-tuple-element.690), channel_id=1, source_target_pairs={{0,8},{8,16},{16,24},{1,9},{9,17},{17,25},{2,10},{10,18},{18,26},{... | collective-permute-start | bytes 786440 | tf_op jit(solution)/shard_map/while/body/eval_jaxpr/ppermute | solution.py:18
  418.7 11.8 %collective-permute-start.1 = (bf16[1,16,8192]{2,1,0:T(8,128)(2,1)}, bf16[1,16,8192]{2,1,0:T(8,128)(2,1)S(1)}, u32[]{:S(2)}, u32[]{:S(2)}) collective-permute-start(bf16[1,16,8192]{2,1,0:T(8,128)(2,1)} %get-tuple-element.706), channel_id=1, source_target_pairs={{8,0},{16,8},{24,16},{9,1},{17,9},{25,17},{10,2},{18,10},{26,18},{... | collective-permute-start | bytes 786440 | tf_op jit(solution)/shard_map/while/body/eval_jaxpr/ppermute | solution.py:18
  433.0 16.0 %collective-permute-start.1 = (bf16[1,16,8192]{2,1,0:T(8,128)(2,1)}, bf16[1,16,8192]{2,1,0:T(8,128)(2,1)S(1)}, u32[]{:S(2)}, u32[]{:S(2)}) collective-permute-start(bf16[1,16,8192]{2,1,0:T(8,128)(2,1)} %get-tuple-element.706), channel_id=1, source_target_pairs={{8,0},{16,8},{24,16},{9,1},{17,9},{25,17},{10,2},{18,10},{26,18},{... | collective-permute-start | bytes 786440 | tf_op jit(solution)/shard_map/while/body/eval_jaxpr/ppermute | solution.py:18
  451.5 88.8 %collective-permute-start.1 = (bf16[1,16,8192]{2,1,0:T(8,128)(2,1)}, bf16[1,16,8192]{2,1,0:T(8,128)(2,1)S(1)}, u32[]{:S(2)}, u32[]{:S(2)}) collective-permute-start(bf16[1,16,8192]{2,1,0:T(8,128)(2,1)} %get-tuple-element.706), channel_id=1, source_target_pairs={{8,0},{16,8},{24,16},{9,1},{17,9},{25,17},{10,2},{18,10},{26,18},{... | collective-permute-start | bytes 786440 | tf_op jit(solution)/shard_map/while/body/eval_jaxpr/ppermute | solution.py:18
  542.3 1.4 copy-start.3
  544.5 0.8 copy-start.1
  546.6 3.6 copy-start.2
  552.7 2.5 copy-start.4
  555.2 10.4 copy-start.6
  569.6 9.4 collective-permute-start.1
  581.0 1.4 copy-start.3
  583.2 0.8 copy-start.1
  585.3 3.6 copy-start.2
  591.4 2.5 copy-start.4
  593.8 10.4 copy-start.6
  608.3 9.4 collective-permute-start.1
  619.6 1.4 copy-start.3
  621.9 0.8 copy-start.1
  624.0 3.6 copy-start.2
  630.0 2.5 copy-start.4
  632.5 10.4 copy-start.6
  647.0 9.4 collective-permute-start.1
  658.3 1.4 copy-start.3
  660.6 0.8 copy-start.1
  662.7 3.6 copy-start.2
  668.7 2.5 copy-start.4
  671.2 10.4 copy-start.6
  685.7 9.4 collective-permute-start.1
  697.0 1.4 copy-start.3
  699.2 0.8 copy-start.1
  701.4 3.6 copy-start.2
  707.4 2.5 copy-start.4
  709.9 10.4 copy-start.6
  724.4 9.4 collective-permute-start.1
  735.7 1.4 copy-start.3
  740.1 3.6 copy-start.2
  746.1 2.5 copy-start.4
  748.6 10.4 copy-start.6
  763.1 9.4 collective-permute-start.1
  774.4 1.4 copy-start.3
  776.6 0.8 copy-start.1
  778.8 3.6 copy-start.2
  784.8 2.5 copy-start.4
  787.3 10.4 copy-start.6
  801.7 9.4 collective-permute-start.1
  813.1 1.4 copy-start.3
  815.3 0.8 copy-start.1
  817.5 3.6 copy-start.2
  823.5 2.5 copy-start.4
  826.0 10.4 copy-start.6
  840.4 8.5 collective-permute-start.1
  (18 other events, 11.3 us)
Sparse Core Ops, SparseCore 0:
  9.6 153.7 all-gather.1
  860.9 165.2 reduce-scatter.1
where the time goes:
time: 1040 us
  waiting for transfers between devices  500 us (48%)
  matrix products  196 us (19%)
  other arithmetic  93.3 us (9%)
  starting transfers between devices  93 us (9%)
  local copies, waits for them, and re-layouts  73.1 us (7%)
  blocking collectives  42.9 us (4%)
  loops' own time  24.8 us (2%)
  between operations  14.7 us (1%)
    ppermute x22, waiting for transfers between devices, from_behind(): return lax.ppermute(shard, axis, pairs)  225 us
    all_gather x1, waiting for transfers between devices, local(): lax.all_gather(kv_weight, 'fsdp', axis=1, tiled=True)  139 us
    reduce_scatter x1, waiting for transfers between devices, local(): lax.psum_scatter(w_term.astype(jnp.bfloat16), 'fsdp', scatter_dimension=0...  135 us
    ppermute x22, starting transfers between devices, from_behind(): return lax.ppermute(shard, axis, pairs)  92.9 us
    dot_general x8, matrix products, backward_layer(): lax.dot_general(flat_dkv, weight, (((1,), (1,)), ((), ())), preferred_ele...  82.8 us
    dot_general x8, matrix products, project(): jnp.dot(flat_rows, weight, preferred_element_type=jnp.float32)  69.5 us
    another operation x64, local copies, waits for them, and re-layouts  31 us
    unnamed x1, blocking collectives  27.2 us
  transfers between devices with their start and end apart: 24, of which 24 were waited for; matrix products, arithmetic and copies ran while one was open for 0% of the time, Pallas kernels for 0%

commit v1 on v0

v1 whole, which is shorter than its diff:
```python
from functools import partial

import jax
import jax.numpy as jnp
from jax import lax
from jax.experimental import pallas as pl
from jax.experimental.pallas import tpu as pltpu
from jax.sharding import PartitionSpec as P

HD = 128
KVH = 4
EPS = 1e-05
BLK = 128


def remote(src, dst, send_sem, recv_sem, device):
    return pltpu.make_async_remote_copy(
        src_ref=src,
        dst_ref=dst,
        send_sem=send_sem,
        recv_sem=recv_sem,
        device_id=device,
        device_id_type=pl.DeviceIdType.MESH,
    )


def nt(a, b):
    return lax.dot_general(a, b, (((1,), (1,)), ((), ())), preferred_element_type=jnp.float32)


def tn(a, b):
    return lax.dot_general(a, b, (((0,), (0,)), ((), ())), preferred_element_type=jnp.float32)


def nn(a, b):
    return jnp.dot(a, b, preferred_element_type=jnp.float32)


def kernel(
    sizes,
    in_ref, cot_ref, w_ref, gain_ref,
    out_w, out_g,
    hbuf, gbuf, wbuf, gains, nbuf, abuf, ubuf, xbuf,
    ssbuf, tbuf, rbuf,
    pbuf, r1, s1, r2, kvbuf,
    dpart, dr1, dkv, dq, gpart,
    nall, dall, gall,
    loc, a_send, a_recv, w_send, w_recv, gn_send, gn_recv,
    ss_send, ss_recv, p1_send, p1_recv, p2_send, p2_recv, p3_send, p3_recv,
    o_send, o_recv,
):
    S, F, mper, seq, df, C, D = sizes
    R = mper * F * seq
    G = F // KVH
    Rg = R // G
    H = df // HD
    NB = R // BLK
    kw = KVH * HD
    scale = HD ** (-0.5)
    me_s, me_f = lax.axis_index("section"), lax.axis_index("fsdp")
    grp, mem = lax.div(me_f, G), lax.rem(me_f, G)

    def fdev(f):
        return {"fsdp": f}

    def sdev(s):
        return {"section": s}

    barrier = pltpu.get_barrier_semaphore()
    for d in range(1, F):
        pl.semaphore_signal(barrier, inc=1, device_id=fdev(lax.rem(me_f + d, F)),
                            device_id_type=pl.DeviceIdType.MESH)
    for d in range(1, S):
        pl.semaphore_signal(barrier, inc=1, device_id=sdev(lax.rem(me_s + d, S)),
                            device_id_type=pl.DeviceIdType.MESH)
    pl.semaphore_wait(barrier, F - 1 + S - 1)

    def rows_of(m, f):
        return pl.ds(pl.multiple_of((m * F + f) * seq, seq), seq)

    def cols_of(f):
        return pl.ds(pl.multiple_of(f * df, df), df)

    def exchange_in(which, src, view):
        sends, recvs = [], []
        for m in range(mper):
            mine = me_s * mper + m
            for d in range(1, F):
                to, frm = lax.rem(me_f + d, F), lax.rem(me_f + F - d, F)
                cp = remote(src.at[mine, :, cols_of(to)], view(rows_of(m, me_f)),
                            a_send.at[which, m, d - 1], a_recv.at[which, m, d - 1], fdev(to))
                cp.start()
                sends.append(cp)
                recvs.append(remote(src.at[mine, :, cols_of(to)], view(rows_of(m, frm)),
                                    a_send.at[which, m, d - 1], a_recv.at[which, m, d - 1],
                                    fdev(to)).wait_recv)
            own = pltpu.make_async_copy(src.at[mine, :, cols_of(me_f)], view(rows_of(m, me_f)),
                                        loc.at[which, m])
            own.start()
            recvs.append(own.wait)
        return sends, recvs

    in_sends, in_recvs = exchange_in(0, in_ref, lambda rows: hbuf.at[0, rows, :])
    own_w = pltpu.make_async_copy(w_ref.at[0], wbuf.at[me_s], loc.at[2, 0])
    own_w.start()
    gains[me_s] = gain_ref[...]
    w_sends = []
    for d in range(1, S):
        to = lax.rem(me_s + d, S)
        cp = remote(gain_ref, gains.at[me_s], gn_send.at[d - 1], gn_recv.at[me_s], sdev(to))
        cp.start()
        w_sends.append(cp)
        cp = remote(w_ref.at[0], wbuf.at[me_s], w_send.at[d - 1], w_recv.at[me_s], sdev(to))
        cp.start()
        w_sends.append(cp)
    cot_sends, cot_recvs = exchange_in(1, cot_ref, lambda rows: gbuf.at[rows, :])

    for wait in in_recvs:
        wait()

    row = lax.broadcasted_iota(jnp.int32, (BLK, BLK), 0)
    col = lax.broadcasted_iota(jnp.int32, (BLK, BLK), 1)
    mask = (row >= col) & (lax.div(row, seq) == lax.div(col, seq))

    def scalars_start(buf, which, l, lanes):
        vec = jnp.sum(jnp.transpose(lanes), axis=0, keepdims=True)
        buf[l, me_f] = jnp.broadcast_to(vec, (8, R))
        for d in range(1, F):
            to = lax.rem(me_f + d, F)
            remote(buf.at[l, me_f], buf.at[l, me_f], ss_send.at[which, l, d - 1],
                   ss_recv.at[which, l, d - 1], fdev(to)).start()

    def scalars_wait(buf, which, l):
        for d in range(1, F):
            to, frm = lax.rem(me_f + d, F), lax.rem(me_f + F - d, F)
            cp = remote(buf.at[l, frm], buf.at[l, frm], ss_send.at[which, l, d - 1],
                        ss_recv.at[which, l, d - 1], fdev(to))
            cp.wait_send()
            cp.wait_recv()
        total = buf[l, 0]
        for f in range(1, F):
            total = total + buf[l, f]
        return total

    def to_column(vec8):
        return jnp.transpose(jnp.broadcast_to(vec8[:1], (HD, R)))

    my_rows = pl.ds(pl.multiple_of(mem * Rg, Rg), Rg)

    def member(j):
        return lax.rem(mem + j, G)

    def mem_rows(m):
        return pl.ds(pl.multiple_of(m * Rg, Rg), Rg)

    def to_owner(kind, l, src, dst):
        @pl.when(l != me_s)
        def _():
            remote(src, dst.at[me_s], o_send.at[kind, l], o_recv.at[kind, me_s], sdev(l)).start()

        @pl.when(l == me_s)
        def _():
            pltpu.make_async_copy(src, dst.at[me_s], o_recv.at[kind, me_s]).start()

    def forward(l, carry):
        acc = jnp.zeros((R, HD), jnp.float32)
        for hh in range(H):
            cs = slice(hh * HD, (hh + 1) * HD)
            v = hbuf[l, :, cs].astype(jnp.float32)
            acc = acc + v * v

        @pl.when(l != me_s)
        def _():
            other = lax.rem(me_s + 1, S)
            remote(gain_ref, gains.at[l], gn_send.at[0], gn_recv.at[l], sdev(other)).wait_recv()
            remote(w_ref.at[0], wbuf.at[l], w_send.at[0], w_recv.at[l], sdev(other)).wait_recv()

        @pl.when(l == me_s)
        def _():
            own_w.wait()

        scalars_start(ssbuf, 0, l, acc)
        gain = gains[l][:1]
        ubuf[...] = (hbuf[l].astype(jnp.float32) * gain).astype(jnp.bfloat16)
        for k in range(KVH):
            pbuf[l, k, :, :HD] = nn(ubuf[...], wbuf[l, :, k * HD:(k + 1) * HD]).astype(jnp.bfloat16)
            pbuf[l, k, :, HD:] = nn(
                ubuf[...], wbuf[l, :, kw + k * HD:kw + (k + 1) * HD]).astype(jnp.bfloat16)
        one = []
        for j in range(1, G):
            cp = remote(pbuf.at[l, :, mem_rows(member(j)), :], r1.at[l, j - 1],
                        p1_send.at[0, l, j - 1], p1_recv.at[0, l, j - 1],
                        fdev(grp * G + member(j)))
            cp.start()
            one.append(cp)
        total = pbuf[l, :, my_rows, :].astype(jnp.float32)
        for j in range(1, G):
            one[j - 1].wait_recv()
            total = total + r1[l, j - 1].astype(jnp.float32)
        s1[l] = total.astype(jnp.bfloat16)
        two = []
        for j in range(1, KVH):
            to = lax.rem(grp + j, KVH)
            cp = remote(s1.at[l, to], r2.at[l, j - 1], p2_send.at[0, l, j - 1],
                        p2_recv.at[0, l, j - 1], fdev(to * G + mem))
            cp.start()
            two.append(cp)
        ss = scalars_wait(ssbuf, 0, l)
        inv = to_column(lax.rsqrt(ss * (1.0 / D) + EPS))
        rbuf[l] = inv
        for hh in range(H):
            cs = slice(hh * HD, (hh + 1) * HD)
            nbuf[l, :, cs] = (
                hbuf[l, :, cs].astype(jnp.float32) * inv * gain[:, cs]).astype(jnp.bfloat16)
        to_owner(0, l, nbuf.at[l], nall)
        kv = s1[l, grp].astype(jnp.float32)
        for j in range(1, KVH):
            two[j - 1].wait_recv()
            kv = kv + r2[l, j - 1].astype(jnp.float32)
        inv_mine = rbuf[l, my_rows, :]
        kvbuf[l, my_rows, :] = jnp.concatenate(
            [kv[:, :HD] * inv_mine, kv[:, HD:] * inv_mine], axis=1).astype(jnp.bfloat16)
        three = []
        for j in range(1, G):
            cp = remote(kvbuf.at[l, my_rows, :], kvbuf.at[l, my_rows, :], p3_send.at[0, l, j - 1],
                        p3_recv.at[0, l, j - 1], fdev(grp * G + member(j)))
            cp.start()
            three.append(cp)
        for j in range(1, G):
            frm = lax.rem(mem + G - j, G)
            remote(kvbuf.at[l, mem_rows(frm), :], kvbuf.at[l, mem_rows(frm), :],
                   p3_send.at[0, l, j - 1], p3_recv.at[0, l, j - 1],
                   fdev(grp * G + member(j))).wait_recv()
        for cp in one + two + three:
            cp.wait_send()
        for b in range(NB):
            rs = slice(b * BLK, (b + 1) * BLK)
            keys, values = kvbuf[l, rs, :HD], kvbuf[l, rs, HD:]
            for hh in range(H):
                cs = slice(hh * HD, (hh + 1) * HD)
                s = jnp.where(mask, nt(nbuf[l, rs, cs], keys) * scale, -1e30)
                e = jnp.exp(s - jnp.max(s, axis=-1, keepdims=True))
                a = e / jnp.sum(e, axis=-1, keepdims=True)
                abuf[l, b * H + hh] = a
                mixed = nn(a.astype(jnp.bfloat16), values)
                hbuf[l + 1, rs, cs] = (
                    hbuf[l, rs, cs].astype(jnp.float32) + mixed).astype(jnp.bfloat16)
        return carry

    lax.fori_loop(0, S, forward, 0)

    for wait in cot_recvs:
        wait()

    def backward(step, carry):
        l = S - 1 - step
        for b in range(NB):
            rs = slice(b * BLK, (b + 1) * BLK)
            keys, values = kvbuf[l, rs, :HD], kvbuf[l, rs, HD:]
            dk = jnp.zeros((BLK, HD), jnp.float32)
            dv = jnp.zeros((BLK, HD), jnp.float32)
            acc = jnp.zeros((BLK, HD), jnp.float32)
            for hh in range(H):
                cs = slice(hh * HD, (hh + 1) * HD)
                a = abuf[l, b * H + hh]
                g = gbuf[rs, cs]
                q = nbuf[l, rs, cs]
                da = nt(g, values)
                ds = a * (da - jnp.sum(da * a, axis=-1, keepdims=True)) * scale
                ds = ds.astype(jnp.bfloat16)
                dqh = nn(ds, keys)
                dq[rs, cs] = dqh
                acc = acc + dqh * q.astype(jnp.float32)
                dk = dk + tn(ds, q)
                dv = dv + tn(a.astype(jnp.bfloat16), g)
            dpart[l, rs, :HD] = dk.astype(jnp.bfloat16)
            dpart[l, rs, HD:] = dv.astype(jnp.bfloat16)
            acc = acc + dk * keys.astype(jnp.float32) + dv * values.astype(jnp.float32)
            xbuf[rs, :] = acc
        one = []
        for j in range(1, G):
            cp = remote(dpart.at[l, mem_rows(member(j)), :], dr1.at[l, j - 1],
                        p1_send.at[1, l, j - 1], p1_recv.at[1, l, j - 1],
                        fdev(grp * G + member(j)))
            cp.start()
            one.append(cp)
        scalars_start(tbuf, 1, l, xbuf[...])
        total = dpart[l, my_rows, :].astype(jnp.float32)
        for j in range(1, G):
            one[j - 1].wait_recv()
            total = total + dr1[l, j - 1].astype(jnp.float32)
        dkv[l, grp, my_rows, :] = total.astype(jnp.bfloat16)
        two = []
        for j in range(1, KVH):
            to, frm = lax.rem(grp + j, KVH), lax.rem(grp + KVH - j, KVH)
            cp = remote(dkv.at[l, grp, my_rows, :], dkv.at[l, grp, my_rows, :],
                        p2_send.at[1, l, j - 1], p2_recv.at[1, l, j - 1], fdev(to * G + mem))
            cp.start()
            two.append(cp)
        for j in range(1, KVH):
            to, frm = lax.rem(grp + j, KVH), lax.rem(grp + KVH - j, KVH)
            remote(dkv.at[l, frm, my_rows, :], dkv.at[l, frm, my_rows, :],
                   p2_send.at[1, l, j - 1], p2_recv.at[1, l, j - 1],
                   fdev(to * G + mem)).wait_recv()
        three = []
        for j in range(1, G):
            cp = remote(dkv.at[l, :, my_rows, :], dkv.at[l, :, my_rows, :],
                        p3_send.at[1, l, j - 1], p3_recv.at[1, l, j - 1],
                        fdev(grp * G + member(j)))
            cp.start()
            three.append(cp)
        t = to_column(scalars_wait(tbuf, 1, l))
        for j in range(1, G):
            frm = lax.rem(mem + G - j, G)
            remote(dkv.at[l, :, mem_rows(frm), :], dkv.at[l, :, mem_rows(frm), :],
                   p3_send.at[1, l, j - 1], p3_recv.at[1, l, j - 1],
                   fdev(grp * G + member(j))).wait_recv()
        for cp in one + two + three:
            cp.wait_send()
        to_owner(1, l, dkv.at[l], dall)
        flat = jnp.concatenate(
            [dkv[l, k, :, :HD] for k in range(KVH)] + [dkv[l, k, :, HD:] for k in range(KVH)],
            axis=1)
        inv = rbuf[l]
        gain = gains[l][:1]
        pull = inv * inv * t * (1.0 / D)
        for hh in range(H):
            cs = slice(hh * HD, (hh + 1) * HD)
            d_total = dq[:, cs] + nt(flat, wbuf[l, cs, :])
            h = hbuf[l, :, cs].astype(jnp.float32)
            gsum = jnp.sum(d_total * (h * inv), axis=0, keepdims=True)
            gpart[l, :, cs] = jnp.broadcast_to(gsum, (8, HD))
            gbuf[:, cs] = (gbuf[:, cs].astype(jnp.float32)
                           + (d_total * (inv * gain[:, cs]) - h * pull)).astype(jnp.bfloat16)
        to_owner(2, l, gpart.at[l], gall)
        return carry

    lax.fori_loop(0, S, backward, 0)

    bufs = ((nbuf, nall), (dkv, dall), (gpart, gall))
    for kind, (src, dst) in enumerate(bufs):
        for s in range(S):
            @pl.when(s != me_s)
            def _():
                cp = remote(src.at[s], dst.at[s], o_send.at[kind, s], o_recv.at[kind, s], sdev(s))
                cp.wait_send()
                cp.wait_recv()

            @pl.when(s == me_s)
            def _():
                pltpu.make_async_copy(src.at[s], dst.at[s], o_recv.at[kind, s]).wait()
    for cp in in_sends + cot_sends + w_sends:
        cp.wait_send()

    normed = nall[...].reshape(S * R, df)
    for k in range(KVH):
        grads = tn(normed, dall[:, k].reshape(S * R, 2 * HD))
        out_w[:, k * HD:(k + 1) * HD] = grads[:, :HD]
        out_w[:, kw + k * HD:kw + (k + 1) * HD] = grads[:, HD:]
    total = gall[0]
    for s in range(1, S):
        total = total + gall[s]
    out_g[...] = total


def local(inputs, cotangent, kv_weight, norm_gain):
    S, F = lax.axis_size("section"), lax.axis_size("fsdp")
    M, seq, D = inputs.shape
    df, C = kv_weight.shape[1:]
    mper = M // S
    R = mper * F * seq
    G = F // KVH
    Rg = R // G
    H = df // HD
    gain8 = jnp.broadcast_to(norm_gain.astype(jnp.float32), (8, df))
    bf, f32 = jnp.bfloat16, jnp.float32
    V, DMA = pltpu.VMEM, pltpu.SemaphoreType.DMA
    n1 = max(G - 1, 1)
    scratch = [
        V((S + 1, R, df), bf), V((R, df), bf), V((S, df, C), bf), V((S, 8, df), f32),
        V((S, R, df), bf), V((S, R // BLK * H, BLK, BLK), f32), V((R, df), bf), V((R, HD), f32),
        V((S, F, 8, R), f32), V((S, F, 8, R), f32), V((S, R, HD), f32),
        V((S, KVH, R, 2 * HD), bf), V((S, n1, KVH, Rg, 2 * HD), bf), V((S, KVH, Rg, 2 * HD), bf),
        V((S, KVH - 1, Rg, 2 * HD), bf), V((S, R, 2 * HD), bf),
        V((S, R, 2 * HD), bf), V((S, n1, Rg, 2 * HD), bf), V((S, KVH, R, 2 * HD), bf),
        V((R, df), f32), V((S, 8, df), f32),
        V((S, R, df), bf), V((S, KVH, R, 2 * HD), bf), V((S, 8, df), f32),
        DMA((3, mper)), DMA((2, mper, F - 1)), DMA((2, mper, F - 1)),
        DMA((S - 1,)), DMA((S,)), DMA((S - 1,)), DMA((S,)),
        DMA((2, S, F - 1)), DMA((2, S, F - 1)),
        DMA((2, S, n1)), DMA((2, S, n1)), DMA((2, S, KVH - 1)), DMA((2, S, KVH - 1)),
        DMA((2, S, n1)), DMA((2, S, n1)), DMA((3, S)), DMA((3, S)),
    ]
    any_spec = pl.BlockSpec(memory_space=pl.ANY)
    vmem_spec = pl.BlockSpec(memory_space=pltpu.VMEM)
    w_share, g_share = pl.pallas_call(
        partial(kernel, (S, F, mper, seq, df, C, D)),
        out_shape=(jax.ShapeDtypeStruct((df, C), f32), jax.ShapeDtypeStruct((8, df), f32)),
        in_specs=[any_spec, any_spec, any_spec, vmem_spec],
        out_specs=(vmem_spec, vmem_spec),
        scratch_shapes=scratch,
        compiler_params=pltpu.CompilerParams(
            collective_id=0, has_side_effects=True, vmem_limit_bytes=60 * 1024 * 1024
        ),
    )(inputs, cotangent, kv_weight, gain8)
    return (w_share[None], g_share[:1])


def solution(mesh):
    in_specs = (
        P(None, "fsdp", None),
        P(None, "fsdp", None),
        P("section", "fsdp", None),
        P("section", "fsdp"),
    )
    out_specs = (P("section", "fsdp", None), P("section", "fsdp"))
    return jax.shard_map(local, mesh=mesh, in_specs=in_specs, out_specs=out_specs, check_vma=False)
```

time: 1040 us -> 268 us (0.26)
  waiting for transfers between devices: 500 us -> 0 us
  Pallas kernels: 0 us -> 259 us
  matrix products: 196 us -> 0 us
  starting transfers between devices: 93 us -> 0 us
  other arithmetic: 93.3 us -> 0.69 us
  local copies, waits for them, and re-layouts: 73.1 us -> 6.76 us
  blocking collectives: 42.9 us -> 0 us
  loops' own time: 24.8 us -> 0 us
  between operations: 14.7 us -> 0.64 us
    pallas_call x0 -> x1, Pallas kernels: none -> 259 us  [local(): pl.pallas_call(partial(kernel, (S, F, mper, seq, df, C, D)), out_shape=(j...]
    ppermute x22 -> x0, waiting for transfers between devices: 225 us -> none  [from_behind(): return lax.ppermute(shard, axis, pairs)]
    dot_general x73 -> x0, matrix products: 196 us -> none  [the longest x8 82.8 us: backward_layer(): lax.dot_general(flat_dkv, weight, (((1,), (1,)), ((), ())), preferred_ele...]
    all_gather x1 -> x0, waiting for transfers between devices: 139 us -> none  [local(): lax.all_gather(kv_weight, 'fsdp', axis=1, tiled=True)]
    reduce_scatter x1 -> x0, waiting for transfers between devices: 135 us -> none  [local(): lax.psum_scatter(w_term.astype(jnp.bfloat16), 'fsdp', scatter_dimension=0...]
    ppermute x22 -> x0, starting transfers between devices: 92.9 us -> none  [from_behind(): return lax.ppermute(shard, axis, pairs)]
    another operation x64 -> x0, local copies, waits for them, and re-layouts: 31 us -> none
    convert_element_type x33 -> x0, other arithmetic: 29.7 us -> none  [the longest x8 14.9 us: backward_layer(): d_rows = (grad_out.astype(jnp.float32) + d_rows_f32).astype(jnp.bfloat16)]
  transfers between devices with their start and end apart: 24 -> 0, of which waited for: 24 -> 0; matrix products, arithmetic and copies ran while one was open for 0% -> 0% of each run, Pallas kernels for 0% -> 0%
where the time goes in v1:
time: 268 us; the launch traced here: 267 us
  Pallas kernels  259 us (97%)
  local copies, waits for them, and re-layouts  6.76 us (3%)
    pallas_call x1, Pallas kernels, local(): pl.pallas_call(partial(kernel, (S, F, mper, seq, df, C, D)), out_shape=(j...  259 us

profile of v1, /device:TPU:0, one launch (start us, length us, event | category | flops | bytes accessed | tf_op | source)
XLA Modules:
  0.0 267.3 jit_solution(1428271706209382437)
XLA Ops:
  0.6 0.7 broadcast_in_dim.17
  1.3 0.6 broadcast_in_dim.15.gain_ref
  1.9 259.2 %shard_map.59 = (f32[1024,1024]{1,0:T(8,128)}, f32[8,1024]{1,0:T(8,128)}) custom-call(bf16[8,16,8192]{2,1,0:T(8,128)(2,1)} %in_ref.1, bf16[8,16,8192]{2,1,0:T(8,128)(2,1)} %cot_ref.1, bf16[1,1024,1024]{2,1,0:T(8,128)(2,1)} %w_ref.1, f32[8,1024]{1,0:T(8,128)} %broadcast_in_dim.15.gain_ref), custom_call_target="tpu_custom_call" | custom-call | tf_op jit(solution)/shard_map/pallas_call | solution.py:396
  261.1 1.4 slice.3
  262.5 4.8 %copy.7 = f32[1,1024,1024]{2,1,0:T(8,128)} copy(f32[1,1024,1024]{2,1,0:T(8,128)} %bitcast.2) | data formatting | bytes 8388608

commit v2 on v1

--- a/solution.py
+++ b/solution.py
@@ -110,13 +110,54 @@
         cp = remote(gain_ref, gains.at[me_s], gn_send.at[d - 1], gn_recv.at[me_s], sdev(to))
         cp.start()
         w_sends.append(cp)
-        cp = remote(w_ref.at[0], wbuf.at[me_s], w_send.at[d - 1], w_recv.at[me_s], sdev(to))
-        cp.start()
-        w_sends.append(cp)
+
+    bits = S.bit_length() - 1
+    half = df // 2
+
+    def bit(x, i):
+        return lax.rem(lax.div(x, 2 ** i), 2)
+
+    def flip(x, i):
+        return x + (1 - 2 * bit(x, i)) * 2 ** i
+
+    def half_of(block, h):
+        return wbuf.at[block, pl.ds(h * half, half), :]
+
+    def order(h):
+        return list(range(bits)) if h == 0 else list(range(bits))[::-1]
+
+    def weight_step(step, wait):
+        arriving = []
+        for h in range(2):
+            done, now = order(h)[:step], order(h)[step]
+            for t in range(2 ** step):
+                block = me_s
+                for p, i in enumerate(done):
+                    if (t >> p) & 1:
+                        block = flip(block, i)
+                to = flip(me_s, now)
+                cp = remote(half_of(block, h), half_of(block, h), w_send.at[h, step, t],
+                            w_recv.at[h, block], sdev(to))
+                cp.start()
+                w_sends.append(cp)
+                came = flip(block, now)
+                arriving.append(remote(half_of(came, h), half_of(came, h), w_send.at[h, step, t],
+                                       w_recv.at[h, came], sdev(to)))
+        if wait:
+            return arriving
+        return []
+
+    own_w.wait()
+    arriving = weight_step(0, bits > 1)
     cot_sends, cot_recvs = exchange_in(1, cot_ref, lambda rows: gbuf.at[rows, :])
 
     for wait in in_recvs:
         wait()
+
+    for step in range(1, bits):
+        for cp in arriving:
+            cp.wait_recv()
+        arriving = weight_step(step, step < bits - 1)
 
     row = lax.broadcasted_iota(jnp.int32, (BLK, BLK), 0)
     col = lax.broadcasted_iota(jnp.int32, (BLK, BLK), 1)
@@ -173,11 +214,12 @@
         def _():
             other = lax.rem(me_s + 1, S)
             remote(gain_ref, gains.at[l], gn_send.at[0], gn_recv.at[l], sdev(other)).wait_recv()
-            remote(w_ref.at[0], wbuf.at[l], w_send.at[0], w_recv.at[l], sdev(other)).wait_recv()
-
-        @pl.when(l == me_s)
-        def _():
-            own_w.wait()
+
+        for h in range(2):
+            @pl.when(bit(l, order(h)[-1]) != bit(me_s, order(h)[-1]))
+            def _():
+                remote(half_of(l, h), half_of(l, h), w_send.at[h, 0, 0], w_recv.at[h, l],
+                       sdev(flip(me_s, order(h)[-1]))).wait_recv()
 
         scalars_start(ssbuf, 0, l, acc)
         gain = gains[l][:1]
@@ -386,7 +428,7 @@
         V((R, df), f32), V((S, 8, df), f32),
         V((S, R, df), bf), V((S, KVH, R, 2 * HD), bf), V((S, 8, df), f32),
         DMA((3, mper)), DMA((2, mper, F - 1)), DMA((2, mper, F - 1)),
-        DMA((S - 1,)), DMA((S,)), DMA((S - 1,)), DMA((S,)),
+        DMA((2, S.bit_length() - 1, S // 2)), DMA((2, S)), DMA((S - 1,)), DMA((S,)),
         DMA((2, S, F - 1)), DMA((2, S, F - 1)),
         DMA((2, S, n1)), DMA((2, S, n1)), DMA((2, S, KVH - 1)), DMA((2, S, KVH - 1)),
         DMA((2, S, n1)), DMA((2, S, n1)), DMA((3, S)), DMA((3, S)),

time: 268 us -> 235 us (0.88)
  Pallas kernels: 259 us -> 227 us
    pallas_call x1, Pallas kernels: 259 us -> 227 us  [local(): pl.pallas_call(partial(kernel, (S, F, mper, seq, df, C, D)), out_shape=(j...]
where the time goes in v2:
time: 235 us
  Pallas kernels  227 us (97%)
  local copies, waits for them, and re-layouts  6.76 us (3%)
    pallas_call x1, Pallas kernels, local(): pl.pallas_call(partial(kernel, (S, F, mper, seq, df, C, D)), out_shape=(j...  227 us
    unnamed x1, local copies, waits for them, and re-layouts  4.79 us

profile of v2, /device:TPU:0, one launch (start us, length us, event | category | flops | bytes accessed | tf_op | source)
XLA Modules:
  0.0 235.1 jit_solution(5769483395923224943)
XLA Ops:
  0.6 0.7 broadcast_in_dim.17
  1.3 0.6 broadcast_in_dim.15.gain_ref
  1.9 227.0 %shard_map.59 = (f32[1024,1024]{1,0:T(8,128)}, f32[8,1024]{1,0:T(8,128)}) custom-call(bf16[8,16,8192]{2,1,0:T(8,128)(2,1)} %in_ref.1, bf16[8,16,8192]{2,1,0:T(8,128)(2,1)} %cot_ref.1, bf16[1,1024,1024]{2,1,0:T(8,128)(2,1)} %w_ref.1, f32[8,1024]{1,0:T(8,128)} %broadcast_in_dim.15.gain_ref), custom_call_target="tpu_custom_call" | custom-call | tf_op jit(solution)/shard_map/pallas_call | solution.py:438
  228.9 1.4 slice.3
  230.3 4.8 %copy.7 = f32[1,1024,1024]{2,1,0:T(8,128)} copy(f32[1,1024,1024]{2,1,0:T(8,128)} %bitcast.2) | data formatting | bytes 8388608

commit v3 on v2

--- a/solution.py
+++ b/solution.py
@@ -149,7 +149,6 @@
 
     own_w.wait()
     arriving = weight_step(0, bits > 1)
-    cot_sends, cot_recvs = exchange_in(1, cot_ref, lambda rows: gbuf.at[rows, :])
 
     for wait in in_recvs:
         wait()
@@ -158,6 +157,8 @@
         for cp in arriving:
             cp.wait_recv()
         arriving = weight_step(step, step < bits - 1)
+
+    cot_sends, cot_recvs = exchange_in(1, cot_ref, lambda rows: gbuf.at[rows, :])
 
     row = lax.broadcasted_iota(jnp.int32, (BLK, BLK), 0)
     col = lax.broadcasted_iota(jnp.int32, (BLK, BLK), 1)
@@ -277,16 +278,24 @@
             cp.wait_send()
         for b in range(NB):
             rs = slice(b * BLK, (b + 1) * BLK)
-            keys, values = kvbuf[l, rs, :HD], kvbuf[l, rs, HD:]
+            keys = kvbuf[l, rs, :HD]
             for hh in range(H):
                 cs = slice(hh * HD, (hh + 1) * HD)
                 s = jnp.where(mask, nt(nbuf[l, rs, cs], keys) * scale, -1e30)
                 e = jnp.exp(s - jnp.max(s, axis=-1, keepdims=True))
                 a = e / jnp.sum(e, axis=-1, keepdims=True)
                 abuf[l, b * H + hh] = a
-                mixed = nn(a.astype(jnp.bfloat16), values)
-                hbuf[l + 1, rs, cs] = (
-                    hbuf[l, rs, cs].astype(jnp.float32) + mixed).astype(jnp.bfloat16)
+
+        @pl.when(l < S - 1)
+        def _():
+            for b in range(NB):
+                rs = slice(b * BLK, (b + 1) * BLK)
+                values = kvbuf[l, rs, HD:]
+                for hh in range(H):
+                    cs = slice(hh * HD, (hh + 1) * HD)
+                    mixed = nn(abuf[l, b * H + hh].astype(jnp.bfloat16), values)
+                    hbuf[l + 1, rs, cs] = (
+                        hbuf[l, rs, cs].astype(jnp.float32) + mixed).astype(jnp.bfloat16)
         return carry
 
     lax.fori_loop(0, S, forward, 0)

time: 235 us -> 220 us (0.936)
  Pallas kernels: 227 us -> 212 us
    pallas_call x1, Pallas kernels: 227 us -> 212 us  [local(): pl.pallas_call(partial(kernel, (S, F, mper, seq, df, C, D)), out_shape=(j...]
where the time goes in v3:
time: 220 us
  Pallas kernels  212 us (96%)
  local copies, waits for them, and re-layouts  6.76 us (3%)
    pallas_call x1, Pallas kernels, local(): pl.pallas_call(partial(kernel, (S, F, mper, seq, df, C, D)), out_shape=(j...  212 us
    unnamed x1, local copies, waits for them, and re-layouts  4.79 us

profile of v3, /device:TPU:0, one launch (start us, length us, event | category | flops | bytes accessed | tf_op | source)
XLA Modules:
  0.0 219.8 jit_solution(6163731285634118972)
XLA Ops:
  0.6 0.7 broadcast_in_dim.17
  1.3 0.6 broadcast_in_dim.15.gain_ref
  1.9 211.7 %shard_map.59 = (f32[1024,1024]{1,0:T(8,128)}, f32[8,1024]{1,0:T(8,128)}) custom-call(bf16[8,16,8192]{2,1,0:T(8,128)(2,1)} %in_ref.1, bf16[8,16,8192]{2,1,0:T(8,128)(2,1)} %cot_ref.1, bf16[1,1024,1024]{2,1,0:T(8,128)(2,1)} %w_ref.1, f32[8,1024]{1,0:T(8,128)} %broadcast_in_dim.15.gain_ref), custom_call_target="tpu_custom_call" | custom-call | tf_op jit(solution)/shard_map/pallas_call | solution.py:447
  213.6 1.4 slice.3
  215.0 4.8 %copy.7 = f32[1,1024,1024]{2,1,0:T(8,128)} copy(f32[1,1024,1024]{2,1,0:T(8,128)} %bitcast.2) | data formatting | bytes 8388608
